TPU v7x, 128 devices: a whole 4x4x4 slice. The times are simulated.
128 devices in a mesh: tok: 32 (over y, x, core), col: 4 (over z).
Axes of the slice: x: 4, y: 4, z: 4, core: 2. Of those that a mesh axis runs over, the one named last changes fastest.
Arguments:
- samples: bfloat16 [131072, 1024], P('tok', 'col')
- lengths: int32 [32, 16], replicated, may hold values from 1 to 4065, as said below
- sketch: bfloat16 [1024, 1024], replicated
Outputs:
- latent_basis: float32 [1024, 1024], P('tok', 'col')
Inputs may be any that keep to these rules, and one draw needn't show every extreme that they name: Each buffer's lengths sum to at most 4096; the sums of buffer i and of the buffer half the tok axis away from it add up to exactly 4096.
All inputs are finite; a program needn't handle non-finite values.
Results may differ from a plain program's by a relative error of at most 0.00037.
Values may be sent and summed in bfloat16 or wider, within the bound.
A program may use at most 128 MiB of HBM per device.

v0:
```python
import math

import jax
import jax.numpy as jnp
from jax import lax
from jax.sharding import PartitionSpec as P


def shifted(block, axis, distance):
    devices = range(lax.axis_size(axis))
    route = [((i - distance) % len(devices), i) for i in devices]
    return lax.ppermute(block, axis, route)


def row_weights(counts, capacity_rows, scale_rows):
    seq_ends = jnp.cumsum(counts)
    seq_starts = seq_ends - counts
    position = lax.iota(jnp.int32, capacity_rows)[None, :]
    covered = (position >= seq_starts[:, None]) & (position < seq_ends[:, None])
    per_sequence = lax.rsqrt(1.0 + 4.0 * counts.astype(jnp.float32) / scale_rows)
    return jnp.sum(jnp.where(covered, per_sequence[:, None], jnp.float32(0.0)), axis=0)


def shards(samples, lengths, sketch):
    row_count = samples.shape[0] // 2
    sketch_width = sketch.shape[1]
    tok_count = lax.axis_size("tok")
    my_index = lax.axis_index("tok")
    partner = (my_index + tok_count // 2) % tok_count
    own_lengths = lax.dynamic_index_in_dim(lengths, my_index, 0, keepdims=False)
    far_lengths = lax.dynamic_index_in_dim(lengths, partner, 0, keepdims=False)
    own_weights = row_weights(own_lengths, 2 * row_count, float(row_count))
    far_weights = row_weights(far_lengths, 2 * row_count, float(row_count))
    received = shifted(samples[row_count:], "tok", tok_count // 2)
    offset = jnp.minimum(jnp.sum(own_lengths), row_count)
    padded_rows = jnp.concatenate(
        [samples[:row_count], jnp.zeros_like(samples[:row_count])], axis=0
    )
    local_rows = lax.dynamic_update_slice_in_dim(padded_rows, received, offset, 0)[:row_count]
    padded_weights = jnp.concatenate(
        [own_weights[:row_count], jnp.zeros((row_count,), jnp.float32)]
    )
    local_weights = lax.dynamic_update_slice_in_dim(
        padded_weights, far_weights[row_count:], offset, 0
    )[:row_count]
    product = jnp.dot(
        lax.all_gather(local_rows, "col", axis=1, tiled=True),
        sketch,
        preferred_element_type=jnp.float32,
    )
    sketched = product * local_weights[:, None]
    contract_rows = (((0,), (0,)), ((), ()))
    local_gram = lax.dot_general(
        sketched,
        sketched,
        contract_rows,
        precision=lax.Precision.HIGHEST,
        preferred_element_type=jnp.float32,
    )
    gram_matrix = lax.psum(local_gram, "tok")
    lower_factor = jnp.linalg.cholesky(gram_matrix)
    basis = jax.scipy.linalg.solve_triangular(lower_factor, sketched.T, lower=True).astype(
        jnp.bfloat16
    )
    factor = math.sqrt(sketch_width / (row_count * tok_count))
    projected = lax.psum_scatter(
        jnp.dot(basis, local_rows, preferred_element_type=jnp.float32),
        "tok",
        scatter_dimension=0,
        tiled=True,
    )
    return projected * factor


def solution(mesh):
    in_specs = (P("tok", "col"), P(), P())
    out_specs = P("tok", "col")
    return jax.shard_map(shards, mesh=mesh, in_specs=in_specs, out_specs=out_specs, check_vma=False)
```

profile of v0, /device:TPU:1, one launch (start us, length us, event | category | flops | bytes accessed | tf_op | source)
XLA Modules:
  0.0 729.2 jit_solution(2391361980113952885)
XLA Ops:
  8.0 3.8 collective-permute-start
  14.1 3.0 broadcast_select_fusion
  17.1 17.4 %collective-permute-done = bf16[2048,256]{1,0:T(8,128)(2,1)} collective-permute-done((bf16[2048,256]{1,0:T(8,128)(2,1)S(1)}, bf16[2048,256]{1,0:T(8,128)(2,1)}, u32[]{:S(2)}, u32[]{:S(2)}) %collective-permute-start) | collective-permute-done | bytes 1048608 | tf_op jit(solution)/shard_map/ppermute | solution.py:12
  34.5 5.9 dynamic_update_slice.6
  43.5 53.9 %all-gather.2.cloned.1.call-done = bf16[2048,1024]{1,0:T(8,128)(2,1)} async-done(((bf16[2048,256]{1,0:T(8,128)(2,1)}), bf16[2048,1024]{1,0:T(8,128)(2,1)}) %all-gather.2.cloned.1.call-update) | async-done | bytes 4194320 | tf_op jit(solution)/shard_map/all_gather | solution.py:47
  97.5 6.3 fusion.78
  103.8 3.2 copy-done.3
  107.0 31.0 %fusion = f32[1024,1024]{0,1:T(8,128)} fusion(f32[2048,1024]{1,0:T(8,128)S(1)} %fusion.78, f32[2048]{0:T(1024)S(1)} %slice.279), kind=kOutput, calls=%fused_computation.3 | convolution fusion | flops 25771900928 | bytes 12591104 | tf_op jit(solution)/shard_map/dot_general | solution.py:53
  138.0 7.2 multiply_bitcast_fusion
  145.2 106.0 %all-reduce.3.cloned.1.call-done = f32[1024,1024]{0,1:T(8,128)} async-done(((f32[1024,1024]{0,1:T(8,128)}), f32[1024,1024]{0,1:T(8,128)}) %all-reduce.3.cloned.1.call-update) | async-done | bytes 4194320 | tf_op jit(solution)/shard_map/psum | solution.py:60
  251.2 5.3 copy.15
  256.6 4.4 fusion.10
  263.0 11.7 %cholesky.223 = f32[128,128]{1,0:T(8,128)S(1)} custom-call(f32[128,128]{1,0:T(8,128)S(1)} %cholesky.580), custom_call_target="Cholesky" | custom-call | tf_op jit(solution)/shard_map/jit(cholesky)/cholesky | solution.py:61
  275.4 9.8 %custom-call.63 = f32[1,128,128]{1,2,0:T(8,128)S(1)} custom-call(f32[1,128,128]{2,1,0:T(8,128)S(1)} %get-tuple-element.64), custom_call_target="InvertDiagBlocksLowerTriangular" | custom-call | tf_op jit(solution)/shard_map/jit(cholesky)/cholesky | solution.py:61
  285.2 2.5 cholesky.255
  287.7 2.4 constant_dynamic-update-slice_fusion.25
  291.6 11.9 %cholesky.244 = f32[128,128]{1,0:T(8,128)S(1)} custom-call(f32[128,128]{1,0:T(8,128)S(1)} %cholesky.584), custom_call_target="Cholesky" | custom-call | tf_op jit(solution)/shard_map/jit(cholesky)/cholesky | solution.py:61
  304.8 9.8 %custom-call.64 = f32[1,128,128]{1,2,0:T(8,128)S(1)} custom-call(f32[1,128,128]{2,1,0:T(8,128)S(1)} %get-tuple-element.61), custom_call_target="InvertDiagBlocksLowerTriangular" | custom-call | tf_op jit(solution)/shard_map/jit(cholesky)/cholesky | solution.py:61
  318.0 11.7 %cholesky.468 = f32[128,128]{1,0:T(8,128)S(1)} custom-call(f32[128,128]{1,0:T(8,128)S(1)} %cholesky.589), custom_call_target="Cholesky" | custom-call | tf_op jit(solution)/shard_map/jit(cholesky)/cholesky | solution.py:61
  331.0 9.8 %custom-call.65 = f32[1,128,128]{1,2,0:T(8,128)S(1)} custom-call(f32[1,128,128]{2,1,0:T(8,128)S(1)} %get-tuple-element.58), custom_call_target="InvertDiagBlocksLowerTriangular" | custom-call | tf_op jit(solution)/shard_map/jit(cholesky)/cholesky | solution.py:61
  342.0 2.3 convolution_subtract_fusion.7
  344.4 11.9 %cholesky.487 = f32[128,128]{1,0:T(8,128)S(1)} custom-call(f32[128,128]{1,0:T(8,128)S(1)} %cholesky.594), custom_call_target="Cholesky" | custom-call | tf_op jit(solution)/shard_map/jit(cholesky)/cholesky | solution.py:61
  357.6 9.8 %custom-call.66 = f32[1,128,128]{1,2,0:T(8,128)S(1)} custom-call(f32[1,128,128]{2,1,0:T(8,128)S(1)} %get-tuple-element.55), custom_call_target="InvertDiagBlocksLowerTriangular" | custom-call | tf_op jit(solution)/shard_map/jit(cholesky)/cholesky | solution.py:61
  368.5 2.3 convolution_subtract_fusion.8
  370.9 11.7 %cholesky.506 = f32[128,128]{1,0:T(8,128)S(1)} custom-call(f32[128,128]{1,0:T(8,128)S(1)} %cholesky.599), custom_call_target="Cholesky" | custom-call | tf_op jit(solution)/shard_map/jit(cholesky)/cholesky | solution.py:61
  383.9 10.2 %custom-call.67 = f32[1,128,128]{1,2,0:T(8,128)S(1)} custom-call(f32[1,128,128]{2,1,0:T(8,128)S(1)} %get-tuple-element.52), custom_call_target="InvertDiagBlocksLowerTriangular" | custom-call | tf_op jit(solution)/shard_map/jit(cholesky)/cholesky | solution.py:61
  395.1 2.3 convolution_subtract_fusion.9
  397.4 11.7 %cholesky.526 = f32[128,128]{1,0:T(8,128)S(1)} custom-call(f32[128,128]{1,0:T(8,128)S(1)} %cholesky.604), custom_call_target="Cholesky" | custom-call | tf_op jit(solution)/shard_map/jit(cholesky)/cholesky | solution.py:61
  410.4 9.8 %custom-call.68 = f32[1,128,128]{1,2,0:T(8,128)S(1)} custom-call(f32[1,128,128]{2,1,0:T(8,128)S(1)} %get-tuple-element.49), custom_call_target="InvertDiagBlocksLowerTriangular" | custom-call | tf_op jit(solution)/shard_map/jit(cholesky)/cholesky | solution.py:61
  423.2 11.9 %cholesky.546 = f32[128,128]{1,0:T(8,128)S(1)} custom-call(f32[128,128]{1,0:T(8,128)S(1)} %cholesky.609), custom_call_target="Cholesky" | custom-call | tf_op jit(solution)/shard_map/jit(cholesky)/cholesky | solution.py:61
  436.4 9.8 %custom-call.69 = f32[1,128,128]{1,2,0:T(8,128)S(1)} custom-call(f32[1,128,128]{2,1,0:T(8,128)S(1)} %get-tuple-element.46), custom_call_target="InvertDiagBlocksLowerTriangular" | custom-call | tf_op jit(solution)/shard_map/jit(cholesky)/cholesky | solution.py:61
  448.8 11.7 %cholesky.564 = f32[128,128]{1,0:T(8,128)S(1)} custom-call(f32[128,128]{1,0:T(8,128)S(1)} %convolution_subtract_fusion.11), custom_call_target="Cholesky" | custom-call | tf_op jit(solution)/shard_map/jit(cholesky)/cholesky | solution.py:61
  466.8 4.8 select_select_fusion
  471.6 23.6 %while.1 = (s32[]{:T(128)}, f32[1024,1024]{1,0:T(8,128)}, s32[8,2]{0,1:T(2,128)S(1)}, f32[8,128,128]{2,1,0:T(8,128)S(1)}, s32[]{:T(128)}) while((s32[]{:T(128)}, f32[1024,1024]{1,0:T(8,128)}, s32[8,2]{0,1:T(2,128)S(1)}, f32[8,128,128]{2,1,0:T(8,128)S(1)}, s32[]{:T(128)}) %tuple.57), condition=%wide.while_cond, body=%wide.while_body.sunk | while | flops 2 | bytes 131189 | solution.py:62
  472.3 2.3 bitcast_dynamic-update-slice_fusion.2
  475.2 2.3 bitcast_dynamic-update-slice_fusion.2
  478.2 2.3 bitcast_dynamic-update-slice_fusion.2
  481.2 2.3 bitcast_dynamic-update-slice_fusion.2
  495.2 78.8 %custom-call.70 = f32[8,128,128]{1,2,0:T(8,128)S(1)} custom-call(f32[8,128,128]{2,1,0:T(8,128)S(1)} %get-tuple-element.12), custom_call_target="InvertDiagBlocksLowerTriangular" | custom-call | tf_op jit(solution)/shard_map/jit(_solve_triangular)/triangular_solve | solution.py:62
  574.0 2.3 convert_dynamic-update-slice_fusion.6
  576.3 3.2 convolution_subtract_fusion.4
  581.1 5.0 convolution_subtract_fusion.3
  587.2 6.7 fusion.18
  594.9 7.6 %fusion.21 = f32[128,2048]{0,1:T(8,128)S(1)} fusion(f32[128,2048]{1,0:T(8,128)S(1)} %get-tuple-element.76, f32[128,2048]{1,0:T(8,128)S(1)} %get-tuple-element.74, f32[128,2048]{1,0:T(8,128)S(1)} %get-tuple-element.72, f32[128,2048]{1,0:T(8,128)S(1)} %get-tuple-element.70, f32[1024,2048]{0,1:T(8,128)S(1)} %bitcast.111, f32[1024,1024]{1,0:T(8,128)} %get-tuple-element.133), kind=kOutput, calls=%fused_computation.30 | convolution fusion | flops 1614020608 | bytes 6553600 | tf_op jit(solution)/shard_map/jit(_solve_triangular)/triangular_solve | solution.py:62
  605.3 9.5 %convolution_subtract_fusion.2 = f32[128,2048]{0,1:T(8,128)S(1)} fusion(f32[640,2048]{1,0:T(8,128)S(1)} %get-tuple-element.30, f32[1024,2048]{0,1:T(8,128)S(1)} %bitcast.111, f32[1024,1024]{1,0:T(8,128)} %get-tuple-element.133), kind=kOutput, calls=%fused_computation.27 | convolution fusion | flops 2013528064 | bytes 7667712 | tf_op jit(solution)/shard_map/jit(_solve_triangular)/triangular_solve | solution.py:62
  616.1 11.1 %convolution_subtract_fusion = f32[128,2048]{0,1:T(8,128)S(1)} fusion(f32[768,2048]{1,0:T(8,128)S(1)} %get-tuple-element.27, f32[1024,2048]{0,1:T(8,128)S(1)} %bitcast.111, f32[1024,1024]{1,0:T(8,128)} %get-tuple-element.133), kind=kOutput, calls=%fused_computation.24 | convolution fusion | flops 2416181248 | bytes 8781824 | tf_op jit(solution)/shard_map/jit(_solve_triangular)/triangular_solve | solution.py:62
  628.5 13.4 %convolution_subtract_fusion.1 = f32[128,2048]{0,1:T(8,128)S(1)} fusion(f32[896,2048]{1,0:T(8,128)S(1)} %constant_dynamic-update-slice_fusion.11, f32[1024,2048]{0,1:T(8,128)S(1)} %bitcast.111, f32[1024,1024]{1,0:T(8,128)} %get-tuple-element.133), kind=kOutput, calls=%fused_computation.26 | convolution fusion | flops 2818834432 | bytes 9895936 | tf_op jit(solution)/shard_map/jit(_solve_triangular)/triangular_solve | solution.py:62
  645.3 75.6 %reduce-scatter.2.cloned.1.call-done = f32[32,256]{1,0:T(8,128)} async-done(((f32[1024,256]{1,0:T(8,128)}), f32[32,256]{1,0:T(8,128)}) %reduce-scatter.2.cloned.1.call-update) | async-done | bytes 32784 | tf_op jit(solution)/shard_map/reduce_scatter | solution.py:66
  (109 shorter events, 59.7 us)
Async XLA Ops:
  6.5 90.9 %copy-start = (bf16[1024,1024]{1,0:T(8,128)(2,1)S(1)}, bf16[1024,1024]{1,0:T(8,128)(2,1)}, u32[]{:S(2)}) copy-start(bf16[1024,1024]{1,0:T(8,128)(2,1)} %param.5) | copy-start | bytes 6291460
  6.5 90.9 %all-gather.2.cloned.1.call-start = ((), (), s32[]{:S(2)}) async-start(), calls=%async_computation.1 | async-start | bytes 5242880 | tf_op jit(solution)/shard_map/all_gather | solution.py:47
  8.0 26.5 %collective-permute-start = (bf16[2048,256]{1,0:T(8,128)(2,1)S(1)}, bf16[2048,256]{1,0:T(8,128)(2,1)}, u32[]{:S(2)}, u32[]{:S(2)}) collective-permute-start(bf16[2048,256]{1,0:T(8,128)(2,1)S(1)} %slice.262), channel_id=1, source_target_pairs={{64,0},{68,4},{72,8},{76,12},{80,16},{84,20},{88,24},{92,28},{96,3... | collective-permute-start | bytes 3145736 | tf_op jit(solution)/shard_map/ppermute | solution.py:12
  14.1 29.3 %copy-start.5 = (pred[4096]{0:T(1024)(128)(4,1)S(1)}, pred[4096]{0:T(1024)(128)(4,1)}, u32[]{:S(2)}) copy-start(pred[4096]{0:T(1024)(128)(4,1)} %constant.307.clone.1) | copy-start | bytes 12292
  42.7 208.5 %all-reduce.3.cloned.1.call-start = ((), (), s32[]{:S(2)}) async-start(), calls=%async_computation.2 | async-start | bytes 8388608 | tf_op jit(solution)/shard_map/psum | solution.py:60
  103.7 3.2 copy-start.3
  138.0 582.9 %reduce-scatter.2.cloned.1.call-start = ((), (), s32[]{:S(2)}) async-start(), calls=%async_computation.3 | async-start | bytes 1081344 | tf_op jit(solution)/shard_map/reduce_scatter | solution.py:66
  261.0 2.0 copy-start.2
  576.3 10.8 %slice-start = ((s8[8388608]{0:T(1024)(128)(4,1)}), s8[4194304]{0:T(1024)(128)(4,1)S(1)}, s32[]{:S(2)}) async-start(s8[8388608]{0:T(1024)(128)(4,1)} %bitcast.110), calls=%async_computation.4 | async-start | bytes 8388608
  580.0 7.2 slice-start.1
  628.4 14.6 %copy-start.4 = (bf16[4096,256]{1,0:T(8,128)(2,1)S(1)}, bf16[4096,256]{1,0:T(8,128)(2,1)}, u32[]{:S(2)}) copy-start(bf16[4096,256]{1,0:T(8,128)(2,1)} %dynamic_update_slice.6) | copy-start | bytes 6291460
  641.9 80.3 %copy-start.1 = (bf16[1024,1024]{1,0:T(8,128)(2,1)S(1)}, bf16[1024,1024]{1,0:T(8,128)(2,1)}, u32[]{:S(2)}) copy-start(bf16[1024,1024]{1,0:T(8,128)(2,1)} %param.5) | copy-start | bytes 6291460
Sparse Core Ops, SparseCore 0:
  42.8 54.5 all-gather.1
  138.1 113.0 all-reduce.2
  645.4 75.3 reduce-scatter.1
where the time goes:
time: 735 us; the launch traced here: 729 us
  other arithmetic  275 us (37%)
  waiting for transfers between devices  253 us (34%)
  matrix products  129 us (18%)
  local copies, waits for them, and re-layouts  48.5 us (7%)
  between operations  19.7 us (3%)
    another operation x31, other arithmetic, shards(): lower_factor = jnp.linalg.cholesky(gram_matrix)  173 us
    psum x1, waiting for transfers between devices, shards(): gram_matrix = lax.psum(local_gram, 'tok')  106 us
    another operation x3, other arithmetic, shards(): jax.scipy.linalg.solve_triangular(lower_factor, sketched.T, lower=True)  83.7 us
    reduce_scatter x1, waiting for transfers between devices, shards(): lax.psum_scatter(jnp.dot(basis, local_rows, preferred_element_type=jnp.fl...  75.6 us
    another operation x15, matrix products, shards(): jax.scipy.linalg.solve_triangular(lower_factor, sketched.T, lower=True)  66.4 us
    all_gather x1, waiting for transfers between devices, shards(): lax.all_gather(local_rows, 'col', axis=1, tiled=True)  53.9 us
    dot_general x1, matrix products, shards(): lax.dot_general(sketched, sketched, contract_rows, precision=lax.Precisio...  31 us
    another operation x24, local copies, waits for them, and re-layouts  23.4 us
  transfers between devices with their start and end apart: 4, of which 4 were waited for; matrix products, arithmetic and copies ran while one was open for 2% of the time, Pallas kernels for 0%

commit v1 on v0

v1 whole, which is shorter than its diff:
```python
import math
import functools
import jax, jax.numpy as jnp
from jax import lax
from jax.experimental import pallas as pl
from jax.experimental.pallas import tpu as pltpu
from jax.sharding import PartitionSpec as P

F32, BF16 = jnp.float32, jnp.bfloat16
BLK = 128

def split(x):
    hi = x.astype(BF16)
    return hi, (x - hi.astype(F32)).astype(BF16)

def mm_t(a, b):
    return lax.dot_general(a, b, (((1,), (1,)), ((), ())), preferred_element_type=F32)

def mm3_t(a, b):
    (ah, al), (bh, bl) = a, b
    return mm_t(ah, bh) + (mm_t(ah, bl) + mm_t(al, bh))

def inverse_factor(m):
    n = m.shape[0]
    sub = lax.broadcasted_iota(jnp.int32, (8, n), 0)
    t = (lax.broadcasted_iota(jnp.int32, (n, n), 0) == lax.broadcasted_iota(jnp.int32, (n, n), 1)).astype(F32)
    out = []
    for s in range(n // 8):
        ms, ts = m[:8], t[:8]
        m, t = m[8:], t[8:]
        cols = [jnp.broadcast_to(ms[:, 8 * s + k:8 * s + k + 1], (8, n)) for k in range(8)]
        e = [[jnp.broadcast_to(cols[k][i:i + 1], (8, n)) for k in range(i + 1)] for i in range(8)]
        r = []
        for k in range(8):
            r.append(lax.rsqrt(e[k][k]))
            for i in range(k + 1, 8):
                e[i][k] = e[i][k] * r[k]
                for j in range(k + 1, i + 1):
                    e[i][j] = e[i][j] - e[i][k] * e[j][k]
        u, v = [], []
        w = None
        for k in range(8):
            mk = jnp.broadcast_to(ms[k:k + 1], (8, n))
            tk = jnp.broadcast_to(ts[k:k + 1], (8, n))
            for j in range(k):
                mk = mk - e[k][j] * u[j]
                tk = tk - e[k][j] * v[j]
            u.append(mk * r[k])
            v.append(tk * r[k])
            w = v[k] if w is None else jnp.where(sub == k, v[k], w)
        out.append(w)
        rest = m.shape[0] // 8
        ml, tl = [], []
        for q in range(rest):
            mq, tq = m[8 * q:8 * q + 8], t[8 * q:8 * q + 8]
            c = []
            for k in range(8):
                ck = jnp.broadcast_to(mq[:, 8 * s + k:8 * s + k + 1], (8, n))
                for j in range(k):
                    ck = ck - c[j] * e[k][j]
                c.append(ck * r[k])
            for k in range(8):
                mq = mq - c[k] * u[k]
                tq = tq - c[k] * v[k]
            ml.append(mq)
            tl.append(tq)
        if rest:
            m, t = jnp.concatenate(ml, 0), jnp.concatenate(tl, 0)
    return jnp.concatenate(out, 0)

def chol_body(n, extra, e_ref, lh, ll):
    total = n + extra
    nb = n // BLK
    for b in range(nb):
        r0, r1 = b * BLK, (b + 1) * BLK
        w = split(inverse_factor(e_ref[r0:r1, r0:r1]))
        for c in range(b + 1, nb + 1):
            lo, hi = c * BLK, min((c + 1) * BLK, total)
            x = mm3_t(split(e_ref[lo:hi, r0:r1]), w)
            if c == nb:
                e_ref[lo:hi, r0:r1] = x
            xh, xl = split(x)
            lh[lo:hi, :] = xh
            ll[lo:hi, :] = xl
        for c in range(b + 1, nb):
            lo = c * BLK
            e_ref[lo:total, lo:lo + BLK] -= mm3_t((lh[lo:total], ll[lo:total]), (lh[lo:lo + BLK], ll[lo:lo + BLK]))

def kernel(n, extra, g_ref, c_ref, o_ref, e, lh, ll, sem):
    cg = pltpu.make_async_copy(g_ref, e.at[0:n], sem.at[0])
    cc = pltpu.make_async_copy(c_ref, e.at[n:n + extra], sem.at[1])
    cg.start(); cc.start(); cg.wait(); cc.wait()
    chol_body(n, extra, e, lh, ll)
    o_ref[...] = e[n:n + extra, :]

def solve(g, ct):
    n, extra = g.shape[0], ct.shape[0]
    return pl.pallas_call(
        functools.partial(kernel, n, extra),
        out_shape=jax.ShapeDtypeStruct((extra, n), F32),
        in_specs=[pl.BlockSpec(memory_space=pl.ANY)] * 2,
        out_specs=pl.BlockSpec(memory_space=pltpu.VMEM),
        scratch_shapes=[pltpu.VMEM((n + extra, n), F32), pltpu.VMEM((n + extra, BLK), BF16), pltpu.VMEM((n + extra, BLK), BF16), pltpu.SemaphoreType.DMA((2,))],
        compiler_params=pltpu.CompilerParams(vmem_limit_bytes=48 << 20),
        cost_estimate=pl.CostEstimate(flops=2_000_000_000, bytes_accessed=8 << 20, transcendentals=1024),
    )(g, ct)


def row_weights(counts, capacity_rows, scale_rows):
    seq_ends = jnp.cumsum(counts)
    seq_starts = seq_ends - counts
    position = lax.iota(jnp.int32, capacity_rows)[None, :]
    covered = (position >= seq_starts[:, None]) & (position < seq_ends[:, None])
    per_sequence = lax.rsqrt(1.0 + 4.0 * counts.astype(jnp.float32) / scale_rows)
    return jnp.sum(jnp.where(covered, per_sequence[:, None], jnp.float32(0.0)), axis=0)


def halves(x):
    hi = lax.reduce_precision(x, 8, 7)
    return hi.astype(BF16), (x - hi).astype(BF16)


def shards(samples, lengths, sketch):
    rows = samples.shape[0]
    tok, col = lax.axis_size("tok"), lax.axis_size("col")
    me, mc = lax.axis_index("tok"), lax.axis_index("col")
    mine = lax.all_to_all(samples, "col", split_axis=0, concat_axis=1, tiled=True)
    w = row_weights(lax.dynamic_index_in_dim(lengths, me, 0, keepdims=False), rows, float(rows // 2))
    w = lax.dynamic_slice_in_dim(w, mc * (rows // col), rows // col, 0)
    s = jnp.dot(mine, sketch, preferred_element_type=F32) * w[:, None]
    sh, sl = halves(s)
    over = (((0,), (0,)), ((), ()))
    dot = lambda a, b: lax.dot_general(a, b, over, preferred_element_type=F32)
    gram = dot(sh, sh) + (dot(sh, sl) + dot(sl, sh))
    cross = dot(mine, sh) + dot(mine, sl)
    gram = lax.psum(gram, ("tok", "col"))
    cross = lax.psum_scatter(cross, ("col", "tok"), scatter_dimension=0, tiled=True)
    y = solve(gram, jnp.concatenate([cross, jnp.zeros_like(cross)], 0))
    y = y[:cross.shape[0]] * math.sqrt(sketch.shape[1] / (rows // 2 * tok))
    return lax.all_to_all(y, "tok", split_axis=1, concat_axis=0, tiled=True).T


def solution(mesh):
    in_specs = (P("tok", "col"), P(), P())
    out_specs = P("tok", "col")
    return jax.shard_map(shards, mesh=mesh, in_specs=in_specs, out_specs=out_specs, check_vma=False)
```

time: 735 us -> 923 us (1.26)
  waiting for transfers between devices: 253 us -> 809 us
  other arithmetic: 275 us -> 1.03 us
  matrix products: 129 us -> 22.6 us
  Pallas kernels: 0 us -> 41.6 us
  local copies, waits for them, and re-layouts: 48.5 us -> 8.74 us
  blocking collectives: 0 us -> 13.4 us
    reduce_scatter x1, waiting for transfers between devices: 75.6 us -> 624 us  [shards(): lax.psum_scatter(cross, ('col', 'tok'), scatter_dimension=0, tiled=True)]
    another operation x38 -> x2, other arithmetic: 257 us -> 0.15 us  [the longest x31 173 us: shards(): lower_factor = jnp.linalg.cholesky(gram_matrix)]
    another operation x29 -> x0, matrix products: 89.5 us -> none  [the longest x15 66.4 us: shards(): jax.scipy.linalg.solve_triangular(lower_factor, sketched.T, lower=True)]
    all_gather x1 -> x0, waiting for transfers between devices: 53.9 us -> none  [shards(): lax.all_gather(local_rows, 'col', axis=1, tiled=True)]
    psum x1, waiting for transfers between devices: 106 us -> 160 us  [shards(): gram = lax.psum(gram, ('tok', 'col'))]
    pallas_call x0 -> x1, Pallas kernels: none -> 41.6 us  [solve(): pl.pallas_call(functools.partial(kernel, n, extra), out_shape=jax.ShapeDt...]
    another operation x34 -> x1, local copies, waits for them, and re-layouts: 26 us -> 0.18 us
    all_to_all x0 -> x1, waiting for transfers between devices: none -> 25.1 us  [shards(): lax.all_to_all(samples, 'col', split_axis=0, concat_axis=1, tiled=True)]
  transfers between devices with their start and end apart: 4 -> 3, of which waited for: 4 -> 3; matrix products, arithmetic and copies ran while one was open for 2% -> 1% of each run, Pallas kernels for 0% -> 0%
where the time goes in v1:
time: 923 us; the launch traced here: 917 us
  waiting for transfers between devices  809 us (88%)
  Pallas kernels  41.6 us (5%)
  matrix products  22.6 us (2%)
  between operations  14 us (2%)
  blocking collectives  13.4 us (1%)
    reduce_scatter x1, waiting for transfers between devices, shards(): lax.psum_scatter(cross, ('col', 'tok'), scatter_dimension=0, tiled=True)  624 us
    psum x1, waiting for transfers between devices, shards(): gram = lax.psum(gram, ('tok', 'col'))  160 us
    pallas_call x1, Pallas kernels, solve(): pl.pallas_call(functools.partial(kernel, n, extra), out_shape=jax.ShapeDt...  41.6 us
    all_to_all x1, waiting for transfers between devices, shards(): lax.all_to_all(samples, 'col', split_axis=0, concat_axis=1, tiled=True)  25.1 us
  transfers between devices with their start and end apart: 3, of which 3 were waited for; matrix products, arithmetic and copies ran while one was open for 1% of the time, Pallas kernels for 0%

profile of v1, /device:TPU:1, one launch (start us, length us, event | category | flops | bytes accessed | tf_op | source)
XLA Modules:
  0.0 917.0 jit_solution(4971881648329756714)
XLA Ops:
  6.5 0.0 copy-start
  6.5 0.0 copy-start.3
  6.5 6.0 all-to-all-start
  12.5 0.0 reduce-scatter.2.cloned.1.call-start
  12.5 0.0 copy-done.3
  12.5 0.2 dynamic-slice_bitcast_fusion
  12.7 0.1 reduce
  12.9 0.1 select_reduce_fusion
  13.1 25.1 %all-to-all-done = bf16[4,1024,256]{2,1,0:T(8,128)(2,1)} async-done(((bf16[4,1024,256]{2,1,0:T(8,128)(2,1)}), bf16[4,1024,256]{2,1,0:T(8,128)(2,1)}, u32[]{:S(2)}, u32[]{:S(2)}) %all-to-all-start) | async-done | bytes 2097184 | tf_op jit(solution)/shard_map/all_to_all | solution.py:127
  38.1 4.0 copy.19
  42.1 0.0 copy-done
  42.1 0.0 copy-start.2
  42.1 4.4 fusion
  46.5 0.0 copy-start.6
  46.5 0.0 copy-start.4
  46.5 0.0 copy-done.2
  46.5 2.3 fusion.4
  48.9 0.0 copy-done.6
  48.9 0.0 copy-done.4
  48.9 4.3 add_bitcast_fusion
  53.2 0.0 reduce-scatter.2.cloned.1.call-update
  53.2 0.6 all-reduce.3.cloned.1.call-start
  53.8 0.0 copy-start.7
  53.8 4.8 fusion.3
  58.5 0.0 copy-done.7
  58.5 0.0 copy-start.5
  58.6 2.4 fusion.2
  60.9 0.0 copy-done.5
  60.9 4.4 add_add_fusion
  65.4 0.0 all-reduce.3.cloned.1.call-update
  65.4 624.3 %reduce-scatter.2.cloned.1.call-done = f32[8,1024]{1,0:T(8,128)} async-done(((f32[1024,1024]{1,0:T(8,128)}), f32[8,1024]{1,0:T(8,128)}) %reduce-scatter.2.cloned.1.call-update) | async-done | bytes 32784 | tf_op jit(solution)/shard_map/reduce_scatter | solution.py:137
  689.8 0.8 concatenate.3.c_ref
  690.5 159.6 %all-reduce.3.cloned.1.call-done.g_ref = f32[1024,1024]{1,0:T(8,128)} async-done(((f32[1024,1024]{1,0:T(8,128)}), f32[1024,1024]{1,0:T(8,128)}) %all-reduce.3.cloned.1.call-update) | async-done | bytes 4194320 | tf_op jit(solution)/shard_map/psum | solution.py:136
  850.1 0.0 copy-start.1
  850.1 2.2 copy-done.1
  852.3 41.6 %shard_map.37 = f32[16,1024]{1,0:T(8,128)S(1)} custom-call(f32[1024,1024]{1,0:T(8,128)S(1)} %copy-done.1, f32[16,1024]{1,0:T(8,128)S(1)} %concatenate.3.c_ref), custom_call_target="tpu_custom_call" | custom-call | flops 2000000000 | bytes 8388608 | tf_op jit(solution)/shard_map/pallas_call | solution.py:98
  894.0 0.1 all_to_all.32
  894.1 0.1 copy.28
  894.2 0.1 reshape.47
  894.3 13.4 %all_to_all.38 = f32[32,1,256]{2,1,0:T(1,128)S(1)} all-to-all(f32[32,1,256]{2,1,0:T(1,128)S(1)} %reshape.47), channel_id=1, replica_groups=mesh['tok'=32,'col'=4] {'tok'}, dimensions={0} | all-to-all | bytes 65536 | tf_op jit(solution)/shard_map/all_to_all | solution.py:140
  907.7 0.5 broadcast.23
  908.2 0.7 reduce.3
  908.9 0.1 reshape.48
  909.0 0.7 copy.24
  (6 shorter events, 0.1 us)
Async XLA Ops:
  6.5 35.6 %copy-start = (bf16[1024,1024]{1,0:T(8,128)(2,1)S(1)}, bf16[1024,1024]{1,0:T(8,128)(2,1)}, u32[]{:S(2)}) copy-start(bf16[1024,1024]{1,0:T(8,128)(2,1)} %param.5) | copy-start | bytes 6291460
  6.5 6.0 copy-start.3
  6.5 31.6 %all-to-all-start = ((bf16[4,1024,256]{2,1,0:T(8,128)(2,1)}), bf16[4,1024,256]{2,1,0:T(8,128)(2,1)}, u32[]{:S(2)}, u32[]{:S(2)}) async-start(bf16[4,1024,256]{2,1,0:T(8,128)(2,1)} %bitcast.30), calls=%async_computation | async-start | bytes 4194304 | tf_op jit(solution)/shard_map/all_to_all | solution.py:127
  12.5 677.2 %reduce-scatter.2.cloned.1.call-start = ((), (), s32[]{:S(2)}) async-start(), calls=%async_computation.4 | async-start | bytes 4227072 | tf_op jit(solution)/shard_map/reduce_scatter | solution.py:137
  42.1 4.4 copy-start.2
  46.5 2.4 copy-start.6
  46.5 2.4 copy-start.4
  53.2 796.9 %all-reduce.3.cloned.1.call-start = ((), (), s32[]{:S(2)}) async-start(), calls=%async_computation.3 | async-start | bytes 8388608 | tf_op jit(solution)/shard_map/psum | solution.py:136
  53.8 4.8 copy-start.7
  58.5 2.4 copy-start.5
  850.1 2.2 copy-start.1
Sparse Core Ops, SparseCore 0:
  53.3 636.3 reduce-scatter.1
  695.4 154.6 all-reduce.2
